TPU v7x, 256 devices: a whole 4x4x8 slice. The times are simulated.
256 devices in a mesh: group: 16 (over x_lo, y, core), loop: 16 (over x_hi, z).
Axes of the slice: x: 4 (x_hi: 2, x_lo: 2; x = x_hi * 2 + x_lo), y: 4, z: 8, core: 2. Of those that a mesh axis runs over, the one named last changes fastest.
Arguments:
- images: bfloat16 [32768, 1152], P(('group', 'loop')), may hold values from -1.5 to 1.5
- texts: bfloat16 [32768, 1152], P(('group', 'loop')), may hold values from -1.5 to 1.5
- logit_scale: float32 [1], replicated, may hold values from 80 to 120
- logit_bias: float32 [1], replicated, may hold values from -15 to -12
Outputs:
- loss: float32 [], replicated
- grad_images: float32 [32768, 1152], P(('group', 'loop'))
- grad_texts: float32 [32768, 1152], P(('group', 'loop'))
All inputs are finite; a program needn't handle non-finite values.
Results may differ from a plain program's by a relative error of at most 0.003.
The roundings to bfloat16 on the way count: a program that leaves them out, or rounds other values in their place, can miss the bound.
Values may be sent and summed in bfloat16 or wider, within the bound.
A program may use at most 64 MiB of HBM per device.

v0:
```python
import jax
import jax.numpy as jnp
from jax import lax
from jax.sharding import PartitionSpec as P


def passed_along(block, axis, distance):
    devices = range(lax.axis_size(axis))
    route = [((i - distance) % len(devices), i) for i in devices]
    return lax.ppermute(block, axis, route)


def unit_rows(raw):
    wide = raw.astype(jnp.float32)
    norm = jnp.sqrt(jnp.sum(wide * wide, axis=1, keepdims=True) + 1e-06)
    return (wide / norm, norm)


def back_norm(unit, norm, grad):
    return (grad - unit * jnp.sum(unit * grad, axis=1, keepdims=True)) / norm


def pair_tile(text_rows, image_rows, positive, scale, bias):
    logits = (
        scale
        * lax.dot_general(
            text_rows, image_rows, (((1,), (1,)), ((), ())), preferred_element_type=jnp.float32
        )
        + bias
    )
    sign = jnp.where(positive, 1.0, -1.0).astype(jnp.float32)
    loss_part = jnp.sum(jax.nn.softplus(-sign * logits))
    pair_grad = (-sign * jax.nn.sigmoid(-sign * logits) * scale).astype(jnp.bfloat16)
    image_part = lax.dot_general(
        pair_grad, text_rows, (((0,), (0,)), ((), ())), preferred_element_type=jnp.float32
    )
    return (loss_part, pair_grad, image_part)


def body(images, texts, logit_scale, logit_bias):
    scale = logit_scale[0]
    bias = logit_bias[0]
    rows = images.shape[0]
    width = images.shape[1]
    groups = lax.axis_size("group")
    loops = lax.axis_size("loop")
    half_loop = loops // 2
    group_index = lax.axis_index("group")
    image_unit, image_norm = unit_rows(images)
    text_unit, text_norm = unit_rows(texts)
    image_low = image_unit.astype(jnp.bfloat16)
    text_low = text_unit.astype(jnp.bfloat16)
    text_rows = lax.all_gather(text_low, "group", axis=0, tiled=True)
    block_rows = text_rows.shape[0]
    row_ids = lax.broadcasted_iota(jnp.int32, (block_rows, 1), 0)
    col_ids = lax.broadcasted_iota(jnp.int32, (1, rows), 1)
    diagonal = row_ids == group_index * rows + col_ids
    kept_start = jnp.zeros((block_rows, width), jnp.float32)

    def one_step(step, carry):
        visitor, visitor_grad, kept, loss_acc = carry
        positive = jnp.logical_and(diagonal, step == 0)
        loss_part, pair_grad, image_part = pair_tile(text_rows, visitor, positive, scale, bias)
        kept = kept + jnp.dot(pair_grad, visitor, preferred_element_type=jnp.float32)
        visitor, visitor_grad = (
            passed_along(visitor.astype(jnp.float32), "loop", 1).astype(visitor.dtype),
            passed_along(visitor_grad + image_part, "loop", 1),
        )
        return (visitor, visitor_grad, kept, loss_acc + loss_part)

    start_carry = (
        image_low,
        jnp.zeros((rows, width), jnp.float32),
        kept_start,
        jnp.zeros((), jnp.float32),
    )
    final = lax.fori_loop(0, half_loop, one_step, start_carry)
    carried = final[1]
    kept = final[2]
    loss_acc = final[3]
    image_grad = passed_along(carried, "loop", -half_loop)
    text_grad = lax.psum_scatter(kept, "group", scatter_dimension=0, tiled=True)
    total = lax.psum(loss_acc, ("group", "loop"))
    batch = rows * groups * loops
    loss = total / batch
    return (
        loss,
        back_norm(image_unit, image_norm, image_grad),
        back_norm(text_unit, text_norm, text_grad),
    )


def solution(mesh):
    placed = (P(("group", "loop"), None), P(("group", "loop"), None), P(), P())
    return jax.shard_map(
        body,
        mesh=mesh,
        in_specs=placed,
        out_specs=(P(), P(("group", "loop"), None), P(("group", "loop"), None)),
        check_vma=False,
    )
```

profile of v0, /device:TPU:16, one launch (start us, length us, event | category | flops | bytes accessed | tf_op | source)
XLA Modules:
  0.0 349.9 jit_solution(12519707428048806134)
XLA Ops:
  8.3 1.8 fusion.9
  12.4 41.0 %all-gather.2.cloned.1.call-done = bf16[2048,1152]{1,0:T(8,128)(2,1)} async-done(((bf16[128,1152]{1,0:T(8,128)(2,1)}), bf16[2048,1152]{1,0:T(8,128)(2,1)}) %all-gather.2.cloned.1.call-update) | async-done | bytes 4718608 | tf_op jit(solution)/shard_map/all_gather | solution.py:53
  53.5 200.5 %while.20 = (s32[]{:T(128)}, bf16[128,1152]{1,0:T(8,128)(2,1)S(1)}, f32[128,1152]{1,0:T(8,128)S(1)}, f32[2048,1152]{1,0:T(8,128)}, f32[]{:T(128)}, /*index=5*/f3...) while((s32[]{:T(128)}, bf16[128,1152]{1,0:T(8,128)(2,1)S(1)}, ...), condition=%wide.region_4.5_spmd.clone, body=%wide.region_2.4_spmd.clone.sunk | while | flops 1825718272 | bytes 51513112 | solution.py:77
  55.1 6.9 %fusion.23 = (f32[]{:T(128)}, f32[2048,128]{1,0:T(8,128)S(1)}) fusion(f32[]{:T(128)} %get-tuple-element.303, bf16[2048,1152]{1,0:T(8,128)(2,1)} %get-tuple-element.302, bf16[128,1152]{1,0:T(8,128)(2,1)S(1)} %copy.13, f32[]{:T(128)} %get-tuple-element.301, pred[]{:T(512)S(6)} %eq.71, s32[128]{0:T(128)S(1)} %get-tuple-element.304), kind=kOutput, calls=%fused_computation.7.clone.1 | convolution fusion | flops 607649792 | bytes 6062605 | tf_op jit(solution)/shard_map/while/body/eval_jaxpr/dot_general | solution.py:26
  65.5 5.9 %convolution_add_fusion.5 = f32[2048,1152]{1,0:T(8,128)} fusion(bf16[128,1152]{1,0:T(8,128)(2,1)S(1)} %copy.13, f32[2048,1152]{1,0:T(8,128)} %get-tuple-element.288, pred[]{:T(512)S(6)} %eq.71, f32[2048,128]{1,0:T(8,128)S(1)} %get-tuple-element.272, s32[128]{0:T(128)S(1)} %get-tuple-element.304, f32[]{:T(128)} %get-tuple-element.301), kind=kOutput, calls=%fused_computation.1.clone.1 | convolution fusion | flops 611319808 | bytes 20218372 | tf_op jit(solution)/shard_map/while/body/eval_jaxpr/dot_general | solution.py:64
  72.0 10.7 %collective-permute-done.1 = f32[128,1152]{1,0:T(8,128)S(1)} collective-permute-done((f32[128,1152]{1,0:T(8,128)S(1)}, f32[128,1152]{1,0:T(8,128)S(1)}, u32[]{:S(2)}, u32[]{:S(2)}) %collective-permute-start.1) | collective-permute-done | bytes 589856 | tf_op jit(solution)/shard_map/while/body/eval_jaxpr/ppermute | solution.py:10
  82.8 6.9 %fusion.23 = (f32[]{:T(128)}, f32[2048,128]{1,0:T(8,128)S(1)}) fusion(f32[]{:T(128)} %get-tuple-element.303, bf16[2048,1152]{1,0:T(8,128)(2,1)} %get-tuple-element.302, bf16[128,1152]{1,0:T(8,128)(2,1)S(1)} %copy.13, f32[]{:T(128)} %get-tuple-element.301, pred[]{:T(512)S(6)} %eq.71, s32[128]{0:T(128)S(1)} %get-tuple-element.304), kind=kOutput, calls=%fused_computation.7.clone.1 | convolution fusion | flops 607649792 | bytes 6062605 | tf_op jit(solution)/shard_map/while/body/eval_jaxpr/dot_general | solution.py:26
  91.6 9.5 %convolution_add_fusion.5 = f32[2048,1152]{1,0:T(8,128)} fusion(bf16[128,1152]{1,0:T(8,128)(2,1)S(1)} %copy.13, f32[2048,1152]{1,0:T(8,128)} %get-tuple-element.288, pred[]{:T(512)S(6)} %eq.71, f32[2048,128]{1,0:T(8,128)S(1)} %get-tuple-element.272, s32[128]{0:T(128)S(1)} %get-tuple-element.304, f32[]{:T(128)} %get-tuple-element.301), kind=kOutput, calls=%fused_computation.1.clone.1 | convolution fusion | flops 611319808 | bytes 20218372 | tf_op jit(solution)/shard_map/while/body/eval_jaxpr/dot_general | solution.py:64
  101.8 7.7 %collective-permute-done.1 = f32[128,1152]{1,0:T(8,128)S(1)} collective-permute-done((f32[128,1152]{1,0:T(8,128)S(1)}, f32[128,1152]{1,0:T(8,128)S(1)}, u32[]{:S(2)}, u32[]{:S(2)}) %collective-permute-start.1) | collective-permute-done | bytes 589856 | tf_op jit(solution)/shard_map/while/body/eval_jaxpr/ppermute | solution.py:10
  109.7 6.9 %fusion.23 = (f32[]{:T(128)}, f32[2048,128]{1,0:T(8,128)S(1)}) fusion(f32[]{:T(128)} %get-tuple-element.303, bf16[2048,1152]{1,0:T(8,128)(2,1)} %get-tuple-element.302, bf16[128,1152]{1,0:T(8,128)(2,1)S(1)} %copy.13, f32[]{:T(128)} %get-tuple-element.301, pred[]{:T(512)S(6)} %eq.71, s32[128]{0:T(128)S(1)} %get-tuple-element.304), kind=kOutput, calls=%fused_computation.7.clone.1 | convolution fusion | flops 607649792 | bytes 6062605 | tf_op jit(solution)/shard_map/while/body/eval_jaxpr/dot_general | solution.py:26
  118.5 9.5 %convolution_add_fusion.5 = f32[2048,1152]{1,0:T(8,128)} fusion(bf16[128,1152]{1,0:T(8,128)(2,1)S(1)} %copy.13, f32[2048,1152]{1,0:T(8,128)} %get-tuple-element.288, pred[]{:T(512)S(6)} %eq.71, f32[2048,128]{1,0:T(8,128)S(1)} %get-tuple-element.272, s32[128]{0:T(128)S(1)} %get-tuple-element.304, f32[]{:T(128)} %get-tuple-element.301), kind=kOutput, calls=%fused_computation.1.clone.1 | convolution fusion | flops 611319808 | bytes 20218372 | tf_op jit(solution)/shard_map/while/body/eval_jaxpr/dot_general | solution.py:64
  128.7 6.8 %collective-permute-done.1 = f32[128,1152]{1,0:T(8,128)S(1)} collective-permute-done((f32[128,1152]{1,0:T(8,128)S(1)}, f32[128,1152]{1,0:T(8,128)S(1)}, u32[]{:S(2)}, u32[]{:S(2)}) %collective-permute-start.1) | collective-permute-done | bytes 589856 | tf_op jit(solution)/shard_map/while/body/eval_jaxpr/ppermute | solution.py:10
  135.6 6.9 %fusion.23 = (f32[]{:T(128)}, f32[2048,128]{1,0:T(8,128)S(1)}) fusion(f32[]{:T(128)} %get-tuple-element.303, bf16[2048,1152]{1,0:T(8,128)(2,1)} %get-tuple-element.302, bf16[128,1152]{1,0:T(8,128)(2,1)S(1)} %copy.13, f32[]{:T(128)} %get-tuple-element.301, pred[]{:T(512)S(6)} %eq.71, s32[128]{0:T(128)S(1)} %get-tuple-element.304), kind=kOutput, calls=%fused_computation.7.clone.1 | convolution fusion | flops 607649792 | bytes 6062605 | tf_op jit(solution)/shard_map/while/body/eval_jaxpr/dot_general | solution.py:26
  144.4 9.5 %convolution_add_fusion.5 = f32[2048,1152]{1,0:T(8,128)} fusion(bf16[128,1152]{1,0:T(8,128)(2,1)S(1)} %copy.13, f32[2048,1152]{1,0:T(8,128)} %get-tuple-element.288, pred[]{:T(512)S(6)} %eq.71, f32[2048,128]{1,0:T(8,128)S(1)} %get-tuple-element.272, s32[128]{0:T(128)S(1)} %get-tuple-element.304, f32[]{:T(128)} %get-tuple-element.301), kind=kOutput, calls=%fused_computation.1.clone.1 | convolution fusion | flops 611319808 | bytes 20218372 | tf_op jit(solution)/shard_map/while/body/eval_jaxpr/dot_general | solution.py:64
  154.6 5.9 %collective-permute-done.1 = f32[128,1152]{1,0:T(8,128)S(1)} collective-permute-done((f32[128,1152]{1,0:T(8,128)S(1)}, f32[128,1152]{1,0:T(8,128)S(1)}, u32[]{:S(2)}, u32[]{:S(2)}) %collective-permute-start.1) | collective-permute-done | bytes 589856 | tf_op jit(solution)/shard_map/while/body/eval_jaxpr/ppermute | solution.py:10
  160.6 6.9 %fusion.23 = (f32[]{:T(128)}, f32[2048,128]{1,0:T(8,128)S(1)}) fusion(f32[]{:T(128)} %get-tuple-element.303, bf16[2048,1152]{1,0:T(8,128)(2,1)} %get-tuple-element.302, bf16[128,1152]{1,0:T(8,128)(2,1)S(1)} %copy.13, f32[]{:T(128)} %get-tuple-element.301, pred[]{:T(512)S(6)} %eq.71, s32[128]{0:T(128)S(1)} %get-tuple-element.304), kind=kOutput, calls=%fused_computation.7.clone.1 | convolution fusion | flops 607649792 | bytes 6062605 | tf_op jit(solution)/shard_map/while/body/eval_jaxpr/dot_general | solution.py:26
  169.4 9.5 %convolution_add_fusion.5 = f32[2048,1152]{1,0:T(8,128)} fusion(bf16[128,1152]{1,0:T(8,128)(2,1)S(1)} %copy.13, f32[2048,1152]{1,0:T(8,128)} %get-tuple-element.288, pred[]{:T(512)S(6)} %eq.71, f32[2048,128]{1,0:T(8,128)S(1)} %get-tuple-element.272, s32[128]{0:T(128)S(1)} %get-tuple-element.304, f32[]{:T(128)} %get-tuple-element.301), kind=kOutput, calls=%fused_computation.1.clone.1 | convolution fusion | flops 611319808 | bytes 20218372 | tf_op jit(solution)/shard_map/while/body/eval_jaxpr/dot_general | solution.py:64
  179.6 5.0 %collective-permute-done.1 = f32[128,1152]{1,0:T(8,128)S(1)} collective-permute-done((f32[128,1152]{1,0:T(8,128)S(1)}, f32[128,1152]{1,0:T(8,128)S(1)}, u32[]{:S(2)}, u32[]{:S(2)}) %collective-permute-start.1) | collective-permute-done | bytes 589856 | tf_op jit(solution)/shard_map/while/body/eval_jaxpr/ppermute | solution.py:10
  184.7 6.9 %fusion.23 = (f32[]{:T(128)}, f32[2048,128]{1,0:T(8,128)S(1)}) fusion(f32[]{:T(128)} %get-tuple-element.303, bf16[2048,1152]{1,0:T(8,128)(2,1)} %get-tuple-element.302, bf16[128,1152]{1,0:T(8,128)(2,1)S(1)} %copy.13, f32[]{:T(128)} %get-tuple-element.301, pred[]{:T(512)S(6)} %eq.71, s32[128]{0:T(128)S(1)} %get-tuple-element.304), kind=kOutput, calls=%fused_computation.7.clone.1 | convolution fusion | flops 607649792 | bytes 6062605 | tf_op jit(solution)/shard_map/while/body/eval_jaxpr/dot_general | solution.py:26
  193.5 9.5 %convolution_add_fusion.5 = f32[2048,1152]{1,0:T(8,128)} fusion(bf16[128,1152]{1,0:T(8,128)(2,1)S(1)} %copy.13, f32[2048,1152]{1,0:T(8,128)} %get-tuple-element.288, pred[]{:T(512)S(6)} %eq.71, f32[2048,128]{1,0:T(8,128)S(1)} %get-tuple-element.272, s32[128]{0:T(128)S(1)} %get-tuple-element.304, f32[]{:T(128)} %get-tuple-element.301), kind=kOutput, calls=%fused_computation.1.clone.1 | convolution fusion | flops 611319808 | bytes 20218372 | tf_op jit(solution)/shard_map/while/body/eval_jaxpr/dot_general | solution.py:64
  203.7 4.0 %collective-permute-done.1 = f32[128,1152]{1,0:T(8,128)S(1)} collective-permute-done((f32[128,1152]{1,0:T(8,128)S(1)}, f32[128,1152]{1,0:T(8,128)S(1)}, u32[]{:S(2)}, u32[]{:S(2)}) %collective-permute-start.1) | collective-permute-done | bytes 589856 | tf_op jit(solution)/shard_map/while/body/eval_jaxpr/ppermute | solution.py:10
  207.9 6.9 %fusion.23 = (f32[]{:T(128)}, f32[2048,128]{1,0:T(8,128)S(1)}) fusion(f32[]{:T(128)} %get-tuple-element.303, bf16[2048,1152]{1,0:T(8,128)(2,1)} %get-tuple-element.302, bf16[128,1152]{1,0:T(8,128)(2,1)S(1)} %copy.13, f32[]{:T(128)} %get-tuple-element.301, pred[]{:T(512)S(6)} %eq.71, s32[128]{0:T(128)S(1)} %get-tuple-element.304), kind=kOutput, calls=%fused_computation.7.clone.1 | convolution fusion | flops 607649792 | bytes 6062605 | tf_op jit(solution)/shard_map/while/body/eval_jaxpr/dot_general | solution.py:26
  214.7 1.8 convolution_add_fusion.4
  216.6 9.5 %convolution_add_fusion.5 = f32[2048,1152]{1,0:T(8,128)} fusion(bf16[128,1152]{1,0:T(8,128)(2,1)S(1)} %copy.13, f32[2048,1152]{1,0:T(8,128)} %get-tuple-element.288, pred[]{:T(512)S(6)} %eq.71, f32[2048,128]{1,0:T(8,128)S(1)} %get-tuple-element.272, s32[128]{0:T(128)S(1)} %get-tuple-element.304, f32[]{:T(128)} %get-tuple-element.301), kind=kOutput, calls=%fused_computation.1.clone.1 | convolution fusion | flops 611319808 | bytes 20218372 | tf_op jit(solution)/shard_map/while/body/eval_jaxpr/dot_general | solution.py:64
  226.8 4.0 %collective-permute-done.1 = f32[128,1152]{1,0:T(8,128)S(1)} collective-permute-done((f32[128,1152]{1,0:T(8,128)S(1)}, f32[128,1152]{1,0:T(8,128)S(1)}, u32[]{:S(2)}, u32[]{:S(2)}) %collective-permute-start.1) | collective-permute-done | bytes 589856 | tf_op jit(solution)/shard_map/while/body/eval_jaxpr/ppermute | solution.py:10
  230.9 6.9 %fusion.23 = (f32[]{:T(128)}, f32[2048,128]{1,0:T(8,128)S(1)}) fusion(f32[]{:T(128)} %get-tuple-element.303, bf16[2048,1152]{1,0:T(8,128)(2,1)} %get-tuple-element.302, bf16[128,1152]{1,0:T(8,128)(2,1)S(1)} %copy.13, f32[]{:T(128)} %get-tuple-element.301, pred[]{:T(512)S(6)} %eq.71, s32[128]{0:T(128)S(1)} %get-tuple-element.304), kind=kOutput, calls=%fused_computation.7.clone.1 | convolution fusion | flops 607649792 | bytes 6062605 | tf_op jit(solution)/shard_map/while/body/eval_jaxpr/dot_general | solution.py:26
  237.8 1.8 convolution_add_fusion.4
  239.7 9.5 %convolution_add_fusion.5 = f32[2048,1152]{1,0:T(8,128)} fusion(bf16[128,1152]{1,0:T(8,128)(2,1)S(1)} %copy.13, f32[2048,1152]{1,0:T(8,128)} %get-tuple-element.288, pred[]{:T(512)S(6)} %eq.71, f32[2048,128]{1,0:T(8,128)S(1)} %get-tuple-element.272, s32[128]{0:T(128)S(1)} %get-tuple-element.304, f32[]{:T(128)} %get-tuple-element.301), kind=kOutput, calls=%fused_computation.1.clone.1 | convolution fusion | flops 611319808 | bytes 20218372 | tf_op jit(solution)/shard_map/while/body/eval_jaxpr/dot_general | solution.py:64
  249.9 4.1 %collective-permute-done.1 = f32[128,1152]{1,0:T(8,128)S(1)} collective-permute-done((f32[128,1152]{1,0:T(8,128)S(1)}, f32[128,1152]{1,0:T(8,128)S(1)}, u32[]{:S(2)}, u32[]{:S(2)}) %collective-permute-start.1) | collective-permute-done | bytes 589856 | tf_op jit(solution)/shard_map/while/body/eval_jaxpr/ppermute | solution.py:10
  254.0 2.8 collective-permute-start.2
  256.8 79.8 %psum.7 = f32[]{:T(128)} all-reduce(f32[]{:T(128)} %get-tuple-element.159), channel_id=1, replica_groups=mesh['group'=16,'loop'=16] {'group','loop'}, use_global_device_ids=true, to_apply=%region_5.6 | all-reduce | flops 1 | bytes 8 | tf_op jit(solution)/shard_map/psum | solution.py:83
  339.8 2.1 subtract_divide_fusion
  (99 shorter events, 21.5 us)
Async XLA Ops:
  7.2 46.3 %all-gather.2.cloned.1.call-start = ((), (), s32[]{:S(2)}) async-start(), calls=%async_computation.1 | async-start | bytes 5013504 | tf_op jit(solution)/shard_map/all_gather | solution.py:53
  10.2 328.4 %reduce-scatter.2.cloned.1.call-start = ((), (), s32[]{:S(2)}) async-start(), calls=%async_computation.2 | async-start | bytes 10027008 | tf_op jit(solution)/shard_map/reduce_scatter | solution.py:82
  53.5 18.5 %collective-permute-start = (bf16[128,1152]{1,0:T(8,128)(2,1)S(1)}, bf16[128,1152]{1,0:T(8,128)(2,1)S(1)}, u32[]{:S(2)}, u32[]{:S(2)}) collective-permute-start(bf16[128,1152]{1,0:T(8,128)(2,1)S(1)} %copy.13), channel_id=1, source_target_pairs={{15,0},{0,1},{1,2},{2,3},{3,4},{4,5},{5,6},{6,7},{7,8},{8,9},{9,10... | collective-permute-start | bytes 884744 | tf_op jit(solution)/shard_map/while/body/eval_jaxpr/ppermute | solution.py:10
  63.8 18.9 %collective-permute-start.1 = (f32[128,1152]{1,0:T(8,128)S(1)}, f32[128,1152]{1,0:T(8,128)S(1)}, u32[]{:S(2)}, u32[]{:S(2)}) collective-permute-start(f32[128,1152]{1,0:T(8,128)S(1)} %convolution_add_fusion.4), channel_id=1, source_target_pairs={{15,0},{0,1},{1,2},{2,3},{3,4},{4,5},{5,6},{6,7},{7,8},{8,9},{9,10... | collective-permute-start | bytes 1769480 | tf_op jit(solution)/shard_map/while/body/eval_jaxpr/ppermute | solution.py:10
  82.7 19.1 %collective-permute-start = (bf16[128,1152]{1,0:T(8,128)(2,1)S(1)}, bf16[128,1152]{1,0:T(8,128)(2,1)S(1)}, u32[]{:S(2)}, u32[]{:S(2)}) collective-permute-start(bf16[128,1152]{1,0:T(8,128)(2,1)S(1)} %copy.13), channel_id=1, source_target_pairs={{15,0},{0,1},{1,2},{2,3},{3,4},{4,5},{5,6},{6,7},{7,8},{8,9},{9,10... | collective-permute-start | bytes 884744 | tf_op jit(solution)/shard_map/while/body/eval_jaxpr/ppermute | solution.py:10
  82.8 6.9 %slice-start = ((s8[4718592]{0:T(1024)(128)(4,1)}), s8[4194304]{0:T(1024)(128)(4,1)S(1)}, s32[]{:S(2)}) async-start(s8[4718592]{0:T(1024)(128)(4,1)} %bitcast.14), calls=%async_computation.3 | async-start | bytes 8388608 | tf_op jit(solution)/shard_map/while
  82.8 6.9 %slice-start.1 = ((s8[4718592]{0:T(1024)(128)(4,1)}), s8[524288]{0:T(1024)(128)(4,1)S(1)}, s32[]{:S(2)}) async-start(s8[4718592]{0:T(1024)(128)(4,1)} %bitcast.14), calls=%async_computation.4 | async-start | bytes 1048576 | tf_op jit(solution)/shard_map/while
  91.5 18.0 %collective-permute-start.1 = (f32[128,1152]{1,0:T(8,128)S(1)}, f32[128,1152]{1,0:T(8,128)S(1)}, u32[]{:S(2)}, u32[]{:S(2)}) collective-permute-start(f32[128,1152]{1,0:T(8,128)S(1)} %convolution_add_fusion.4), channel_id=1, source_target_pairs={{15,0},{0,1},{1,2},{2,3},{3,4},{4,5},{5,6},{6,7},{7,8},{8,9},{9,10... | collective-permute-start | bytes 1769480 | tf_op jit(solution)/shard_map/while/body/eval_jaxpr/ppermute | solution.py:10
  109.6 19.1 %collective-permute-start = (bf16[128,1152]{1,0:T(8,128)(2,1)S(1)}, bf16[128,1152]{1,0:T(8,128)(2,1)S(1)}, u32[]{:S(2)}, u32[]{:S(2)}) collective-permute-start(bf16[128,1152]{1,0:T(8,128)(2,1)S(1)} %copy.13), channel_id=1, source_target_pairs={{15,0},{0,1},{1,2},{2,3},{3,4},{4,5},{5,6},{6,7},{7,8},{8,9},{9,10... | collective-permute-start | bytes 884744 | tf_op jit(solution)/shard_map/while/body/eval_jaxpr/ppermute | solution.py:10
  109.7 6.9 %slice-start = ((s8[4718592]{0:T(1024)(128)(4,1)}), s8[4194304]{0:T(1024)(128)(4,1)S(1)}, s32[]{:S(2)}) async-start(s8[4718592]{0:T(1024)(128)(4,1)} %bitcast.14), calls=%async_computation.3 | async-start | bytes 8388608 | tf_op jit(solution)/shard_map/while
  109.7 6.9 %slice-start.1 = ((s8[4718592]{0:T(1024)(128)(4,1)}), s8[524288]{0:T(1024)(128)(4,1)S(1)}, s32[]{:S(2)}) async-start(s8[4718592]{0:T(1024)(128)(4,1)} %bitcast.14), calls=%async_computation.4 | async-start | bytes 1048576 | tf_op jit(solution)/shard_map/while
  118.4 17.1 %collective-permute-start.1 = (f32[128,1152]{1,0:T(8,128)S(1)}, f32[128,1152]{1,0:T(8,128)S(1)}, u32[]{:S(2)}, u32[]{:S(2)}) collective-permute-start(f32[128,1152]{1,0:T(8,128)S(1)} %convolution_add_fusion.4), channel_id=1, source_target_pairs={{15,0},{0,1},{1,2},{2,3},{3,4},{4,5},{5,6},{6,7},{7,8},{8,9},{9,10... | collective-permute-start | bytes 1769480 | tf_op jit(solution)/shard_map/while/body/eval_jaxpr/ppermute | solution.py:10
  135.5 19.1 %collective-permute-start = (bf16[128,1152]{1,0:T(8,128)(2,1)S(1)}, bf16[128,1152]{1,0:T(8,128)(2,1)S(1)}, u32[]{:S(2)}, u32[]{:S(2)}) collective-permute-start(bf16[128,1152]{1,0:T(8,128)(2,1)S(1)} %copy.13), channel_id=1, source_target_pairs={{15,0},{0,1},{1,2},{2,3},{3,4},{4,5},{5,6},{6,7},{7,8},{8,9},{9,10... | collective-permute-start | bytes 884744 | tf_op jit(solution)/shard_map/while/body/eval_jaxpr/ppermute | solution.py:10
  135.6 6.9 %slice-start = ((s8[4718592]{0:T(1024)(128)(4,1)}), s8[4194304]{0:T(1024)(128)(4,1)S(1)}, s32[]{:S(2)}) async-start(s8[4718592]{0:T(1024)(128)(4,1)} %bitcast.14), calls=%async_computation.3 | async-start | bytes 8388608 | tf_op jit(solution)/shard_map/while
  135.6 6.9 %slice-start.1 = ((s8[4718592]{0:T(1024)(128)(4,1)}), s8[524288]{0:T(1024)(128)(4,1)S(1)}, s32[]{:S(2)}) async-start(s8[4718592]{0:T(1024)(128)(4,1)} %bitcast.14), calls=%async_computation.4 | async-start | bytes 1048576 | tf_op jit(solution)/shard_map/while
  144.3 16.2 %collective-permute-start.1 = (f32[128,1152]{1,0:T(8,128)S(1)}, f32[128,1152]{1,0:T(8,128)S(1)}, u32[]{:S(2)}, u32[]{:S(2)}) collective-permute-start(f32[128,1152]{1,0:T(8,128)S(1)} %convolution_add_fusion.4), channel_id=1, source_target_pairs={{15,0},{0,1},{1,2},{2,3},{3,4},{4,5},{5,6},{6,7},{7,8},{8,9},{9,10... | collective-permute-start | bytes 1769480 | tf_op jit(solution)/shard_map/while/body/eval_jaxpr/ppermute | solution.py:10
  160.5 19.1 %collective-permute-start = (bf16[128,1152]{1,0:T(8,128)(2,1)S(1)}, bf16[128,1152]{1,0:T(8,128)(2,1)S(1)}, u32[]{:S(2)}, u32[]{:S(2)}) collective-permute-start(bf16[128,1152]{1,0:T(8,128)(2,1)S(1)} %copy.13), channel_id=1, source_target_pairs={{15,0},{0,1},{1,2},{2,3},{3,4},{4,5},{5,6},{6,7},{7,8},{8,9},{9,10... | collective-permute-start | bytes 884744 | tf_op jit(solution)/shard_map/while/body/eval_jaxpr/ppermute | solution.py:10
  160.6 6.9 %slice-start = ((s8[4718592]{0:T(1024)(128)(4,1)}), s8[4194304]{0:T(1024)(128)(4,1)S(1)}, s32[]{:S(2)}) async-start(s8[4718592]{0:T(1024)(128)(4,1)} %bitcast.14), calls=%async_computation.3 | async-start | bytes 8388608 | tf_op jit(solution)/shard_map/while
  160.6 6.9 %slice-start.1 = ((s8[4718592]{0:T(1024)(128)(4,1)}), s8[524288]{0:T(1024)(128)(4,1)S(1)}, s32[]{:S(2)}) async-start(s8[4718592]{0:T(1024)(128)(4,1)} %bitcast.14), calls=%async_computation.4 | async-start | bytes 1048576 | tf_op jit(solution)/shard_map/while
  169.3 15.3 %collective-permute-start.1 = (f32[128,1152]{1,0:T(8,128)S(1)}, f32[128,1152]{1,0:T(8,128)S(1)}, u32[]{:S(2)}, u32[]{:S(2)}) collective-permute-start(f32[128,1152]{1,0:T(8,128)S(1)} %convolution_add_fusion.4), channel_id=1, source_target_pairs={{15,0},{0,1},{1,2},{2,3},{3,4},{4,5},{5,6},{6,7},{7,8},{8,9},{9,10... | collective-permute-start | bytes 1769480 | tf_op jit(solution)/shard_map/while/body/eval_jaxpr/ppermute | solution.py:10
  184.6 19.1 %collective-permute-start = (bf16[128,1152]{1,0:T(8,128)(2,1)S(1)}, bf16[128,1152]{1,0:T(8,128)(2,1)S(1)}, u32[]{:S(2)}, u32[]{:S(2)}) collective-permute-start(bf16[128,1152]{1,0:T(8,128)(2,1)S(1)} %copy.13), channel_id=1, source_target_pairs={{15,0},{0,1},{1,2},{2,3},{3,4},{4,5},{5,6},{6,7},{7,8},{8,9},{9,10... | collective-permute-start | bytes 884744 | tf_op jit(solution)/shard_map/while/body/eval_jaxpr/ppermute | solution.py:10
  184.7 6.9 %slice-start = ((s8[4718592]{0:T(1024)(128)(4,1)}), s8[4194304]{0:T(1024)(128)(4,1)S(1)}, s32[]{:S(2)}) async-start(s8[4718592]{0:T(1024)(128)(4,1)} %bitcast.14), calls=%async_computation.3 | async-start | bytes 8388608 | tf_op jit(solution)/shard_map/while
  193.4 14.3 %collective-permute-start.1 = (f32[128,1152]{1,0:T(8,128)S(1)}, f32[128,1152]{1,0:T(8,128)S(1)}, u32[]{:S(2)}, u32[]{:S(2)}) collective-permute-start(f32[128,1152]{1,0:T(8,128)S(1)} %convolution_add_fusion.4), channel_id=1, source_target_pairs={{15,0},{0,1},{1,2},{2,3},{3,4},{4,5},{5,6},{6,7},{7,8},{8,9},{9,10... | collective-permute-start | bytes 1769480 | tf_op jit(solution)/shard_map/while/body/eval_jaxpr/ppermute | solution.py:10
  207.7 19.1 %collective-permute-start = (bf16[128,1152]{1,0:T(8,128)(2,1)S(1)}, bf16[128,1152]{1,0:T(8,128)(2,1)S(1)}, u32[]{:S(2)}, u32[]{:S(2)}) collective-permute-start(bf16[128,1152]{1,0:T(8,128)(2,1)S(1)} %copy.13), channel_id=1, source_target_pairs={{15,0},{0,1},{1,2},{2,3},{3,4},{4,5},{5,6},{6,7},{7,8},{8,9},{9,10... | collective-permute-start | bytes 884744 | tf_op jit(solution)/shard_map/while/body/eval_jaxpr/ppermute | solution.py:10
  207.8 6.9 %slice-start = ((s8[4718592]{0:T(1024)(128)(4,1)}), s8[4194304]{0:T(1024)(128)(4,1)S(1)}, s32[]{:S(2)}) async-start(s8[4718592]{0:T(1024)(128)(4,1)} %bitcast.14), calls=%async_computation.3 | async-start | bytes 8388608 | tf_op jit(solution)/shard_map/while
  216.5 14.3 %collective-permute-start.1 = (f32[128,1152]{1,0:T(8,128)S(1)}, f32[128,1152]{1,0:T(8,128)S(1)}, u32[]{:S(2)}, u32[]{:S(2)}) collective-permute-start(f32[128,1152]{1,0:T(8,128)S(1)} %convolution_add_fusion.4), channel_id=1, source_target_pairs={{15,0},{0,1},{1,2},{2,3},{3,4},{4,5},{5,6},{6,7},{7,8},{8,9},{9,10... | collective-permute-start | bytes 1769480 | tf_op jit(solution)/shard_map/while/body/eval_jaxpr/ppermute | solution.py:10
  230.8 19.1 %collective-permute-start = (bf16[128,1152]{1,0:T(8,128)(2,1)S(1)}, bf16[128,1152]{1,0:T(8,128)(2,1)S(1)}, u32[]{:S(2)}, u32[]{:S(2)}) collective-permute-start(bf16[128,1152]{1,0:T(8,128)(2,1)S(1)} %copy.13), channel_id=1, source_target_pairs={{15,0},{0,1},{1,2},{2,3},{3,4},{4,5},{5,6},{6,7},{7,8},{8,9},{9,10... | collective-permute-start | bytes 884744 | tf_op jit(solution)/shard_map/while/body/eval_jaxpr/ppermute | solution.py:10
  230.9 6.9 %slice-start = ((s8[4718592]{0:T(1024)(128)(4,1)}), s8[4194304]{0:T(1024)(128)(4,1)S(1)}, s32[]{:S(2)}) async-start(s8[4718592]{0:T(1024)(128)(4,1)} %bitcast.14), calls=%async_computation.3 | async-start | bytes 8388608 | tf_op jit(solution)/shard_map/while
  239.6 14.4 %collective-permute-start.1 = (f32[128,1152]{1,0:T(8,128)S(1)}, f32[128,1152]{1,0:T(8,128)S(1)}, u32[]{:S(2)}, u32[]{:S(2)}) collective-permute-start(f32[128,1152]{1,0:T(8,128)S(1)} %convolution_add_fusion.4), channel_id=1, source_target_pairs={{15,0},{0,1},{1,2},{2,3},{3,4},{4,5},{5,6},{6,7},{7,8},{8,9},{9,10... | collective-permute-start | bytes 1769480 | tf_op jit(solution)/shard_map/while/body/eval_jaxpr/ppermute | solution.py:10
  254.0 83.3 %copy-start = (bf16[128,1152]{1,0:T(8,128)(2,1)S(1)}, bf16[128,1152]{1,0:T(8,128)(2,1)}, u32[]{:S(2)}) copy-start(bf16[128,1152]{1,0:T(8,128)(2,1)} %param.6) | copy-start | bytes 884740
  254.0 84.6 %copy-start.1 = (bf16[128,1152]{1,0:T(8,128)(2,1)S(1)}, bf16[128,1152]{1,0:T(8,128)(2,1)}, u32[]{:S(2)}) copy-start(bf16[128,1152]{1,0:T(8,128)(2,1)} %param.7) | copy-start | bytes 884740
  254.0 83.3 %collective-permute-start.2 = (f32[128,1152]{1,0:T(8,128)S(1)}, f32[128,1152]{1,0:T(8,128)S(1)}, u32[]{:S(2)}, u32[]{:S(2)}) collective-permute-start(f32[128,1152]{1,0:T(8,128)S(1)} %get-tuple-element.160), channel_id=1, source_target_pairs={{8,0},{9,1},{10,2},{11,3},{12,4},{13,5},{14,6},{15,7},{0,8},{1,9},... | collective-permute-start | bytes 1769480 | tf_op jit(solution)/shard_map/ppermute | solution.py:10
  (5 other events, 34.5 us)
Sparse Core Ops, SparseCore 0:
  10.4 42.9 all-gather.1
  254.1 70.3 reduce-scatter.1
where the time goes:
time: 354 us; the launch traced here: 350 us
  matrix products  142 us (40%)
  waiting for transfers between devices  89.2 us (25%)
  blocking collectives  79.8 us (23%)
  between operations  15.9 us (4%)
  other arithmetic  9.74 us (3%)
  starting transfers between devices  7.31 us (2%)
  loops' own time  5.64 us (2%)
    psum x1, blocking collectives, body(): total = lax.psum(loss_acc, ('group', 'loop'))  79.8 us
    dot_general x8, matrix products, one_step(): jnp.dot(pair_grad, visitor, preferred_element_type=jnp.float32)  72.7 us
    dot_general x8, matrix products, pair_tile(): lax.dot_general(text_rows, image_rows, (((1,), (1,)), ((), ())), preferre...  55.1 us
    ppermute x17, waiting for transfers between devices, passed_along(): return lax.ppermute(block, axis, route)  48.2 us
    all_gather x1, waiting for transfers between devices, body(): text_rows = lax.all_gather(text_low, 'group', axis=0, tiled=True)  41 us
    dot_general x8, matrix products, pair_tile(): lax.dot_general(pair_grad, text_rows, (((0,), (0,)), ((), ())), preferred...  14.3 us
    ppermute x17, starting transfers between devices, passed_along(): return lax.ppermute(block, axis, route)  7.23 us
  transfers between devices with their start and end apart: 19, of which 9 were waited for; matrix products, arithmetic and copies ran while one was open for 42% of the time, Pallas kernels for 0%

commit v1 on v0

v1 whole, which is shorter than its diff:
```python
import jax
import jax.numpy as jnp
from jax import lax
from jax.experimental import pallas as pl
from jax.experimental.pallas import tpu as pltpu
from jax.sharding import PartitionSpec as P

MESH = pl.DeviceIdType.MESH
F32 = jnp.float32
LOW = jnp.bfloat16
ROWS = 128
HALF = 64
WIDTH = 1152
CHUNK = 4 * ROWS
NT = (((1,), (1,)), ((), ()))
NN = (((1,), (0,)), ((), ()))
TN = (((0,), (0,)), ((), ()))
A, B = 0, 1
(NEXT, PREV, BACK, UNBACK, YUP, YDOWN, YFAR, CORE, LO, MIRROR, XFAR, ZPAIR, ZUP2, ZDOWN2, ZFAR) = range(15)
GREETED = (NEXT, PREV, BACK, UNBACK, YUP, YDOWN, YFAR, CORE, LO, MIRROR, XFAR, ZUP2, ZDOWN2, ZFAR)
(
    F1, F2, F3, F4, B1, B2, B3, B4, S0, S1, S2, S3, S4, S5, S6, S7, G0, G1, G2, G3, G4, G5, G6, G7,
    TU, TD, TX, TXU, TXD, T2U, T2D, T3X, CF0, CF1, CF2, CF3, CB0, CB1, CB2, CB3,
    X1, X2, Y1U, Y1D, Y0U, Y0D, Y3U, Y3D,
    LC, LX, LM, LF, LYU, LYD, LYF, LZ, LZU, LZD, LZF, LAST,
) = range(0, 120, 2)
HALVED = (
    F1, F2, F3, B1, B2, B3, S0, S1, S2, S3, S4, S5, S6, S7, TU, TD, TX, TXU, TXD, T3X,
    CF0, CF1, CF2, CB0, CB1, CB2, X1, X2, Y1U, Y1D, Y0U, Y0D,
)
SENT = (
    [hop + h for hop in HALVED for h in (A, B)]
    + [F4 + A, B4 + B, T2U + A, T2D + B, CF3 + A, CB3 + B, Y3U + A, Y3D + B]
    + list(range(G0, G7 + 1, 2))
    + list(range(LC, LZF + 1, 2))
)
VISITS = {
    F1: (0, 1, NEXT), F2: (1, 3, NEXT), F3: (3, 5, NEXT), F4: (5, 7, NEXT),
    B1: (0, 2, BACK), B2: (2, 4, PREV), B3: (4, 6, PREV), B4: (6, 7, PREV),
}
OWN, SIDE, UP, DOWN, FAR, SIDE_UP, SIDE_DOWN, SIDE_FAR = range(8)
TEXTS = {
    TU: (OWN, DOWN, YUP), TD: (OWN, UP, YDOWN), TX: (OWN, SIDE, LO),
    T2U: (DOWN, FAR, YUP), T2D: (UP, FAR, YDOWN),
    TXU: (SIDE, SIDE_DOWN, YUP), TXD: (SIDE, SIDE_UP, YDOWN), T3X: (FAR, SIDE_FAR, LO),
}
SUMS = {
    CF0: (0, PREV), CF1: (1, PREV), CF2: (2, PREV), CF3: (3, PREV),
    CB0: (4, UNBACK), CB1: (5, NEXT), CB2: (6, NEXT), CB3: (7, NEXT),
    X1: (8, LO), X2: (9, LO), Y1U: (10, YUP), Y1D: (11, YDOWN),
    Y0U: (12, YUP), Y0D: (13, YDOWN), Y3U: (14, YUP), Y3D: (14, YDOWN),
}
LOSSES = {
    LC: (0, 0, CORE), LX: (1, 1, LO), LM: (1, 2, MIRROR), LF: (1, 3, XFAR),
    LYU: (2, 4, YUP), LYD: (2, 5, YDOWN), LYF: (2, 6, YFAR),
    LZ: (3, 7, ZPAIR), LZU: (4, 8, ZUP2), LZD: (4, 9, ZDOWN2), LZF: (4, 10, ZFAR),
}


def dot(a, b, dims):
    return lax.dot_general(a, b, dims, preferred_element_type=F32)


def unit_rows(raw):
    wide = raw.astype(F32)
    norm = jnp.sqrt(jnp.sum(wide * wide, axis=1, keepdims=True) + 1e-06)
    return wide / norm, norm


def back_norm(unit, norm, grad):
    return (grad - unit * jnp.sum(unit * grad, axis=1, keepdims=True)) / norm


def devices():
    g, l = lax.axis_index("group"), lax.axis_index("loop")
    core, y, lo = g % 2, (g // 2) % 4, g // 8
    z, hi = l % 8, l // 8

    def at(lo=lo, y=y, core=core, hi=hi, z=z):
        return ((lo * 4 + y) * 2 + core, hi * 8 + z)

    def flip(bit, when):
        return jnp.where(when, 1 - bit, bit)

    up, down = (z + 1) % 8, (z + 7) % 8
    return {
        NEXT: at(lo=flip(lo, z == 7), hi=flip(hi, z == 7), z=up),
        PREV: at(lo=flip(lo, z == 0), hi=flip(hi, z == 0), z=down),
        BACK: at(lo=flip(lo, z != 0), hi=flip(hi, z != 0), z=down),
        UNBACK: at(lo=flip(lo, z != 7), hi=flip(hi, z != 7), z=up),
        YUP: at(y=(y + 1) % 4),
        YDOWN: at(y=(y + 3) % 4),
        YFAR: at(y=(y + 2) % 4),
        CORE: at(core=1 - core),
        LO: at(lo=1 - lo),
        MIRROR: at(lo=1 - lo, hi=1 - hi),
        XFAR: at(hi=1 - hi),
        ZPAIR: at(z=z + 1 - 2 * (z % 2)),
        ZUP2: at(z=(z + 2) % 8),
        ZDOWN2: at(z=(z + 6) % 8),
        ZFAR: at(z=(z + 4) % 8),
    }


def kernel(
    scale_ref, bias_ref, img_ref, txt_ref, loss_ref, gimg_ref, gtxt_ref,
    raw, unit, V, T, gI, sI, rI, gT, out, arrived, lacc, lout, lin, lsem, ssem, rsem,
):
    dev = devices()
    scale, bias = scale_ref[0], bias_ref[0]
    loads = [pltpu.make_async_copy(ref, raw.at[i], lsem.at[i]) for i, ref in enumerate((img_ref, txt_ref))]
    for load in loads:
        load.start()

    barrier = pltpu.get_barrier_semaphore()
    for to in GREETED:
        pl.semaphore_signal(barrier, inc=1, device_id=dev[to], device_id_type=MESH)

    def rows(i, h):
        return pl.ds(i * ROWS + h * HALF, HALF)

    def copy(name):
        h, base = name % 2, name - name % 2
        if base in VISITS:
            s, d, to = VISITS[base]
            src, dst = V.at[s, rows(0, h)], V.at[d, rows(0, h)]
        elif base in TEXTS:
            s, d, to = TEXTS[base]
            src, dst = T.at[rows(s, h)], T.at[rows(d, h)]
        elif base in SUMS:
            k, to = SUMS[base]
            src, dst = out.at[k, rows(0, h)], arrived.at[k, rows(0, h)]
        elif base in LOSSES:
            s, d, to = LOSSES[base]
            src, dst = lout.at[s], lin.at[d]
        elif base >= G0:
            s, to = (base - G0) // 2, CORE
            src, dst = sI.at[s], rI.at[s]
        else:
            s, to = (base - S0) // 2, CORE
            src, dst = V.at[s, rows(0, h)], V.at[s, rows(1, h)]
        return pltpu.make_async_remote_copy(
            src_ref=src, dst_ref=dst, send_sem=ssem.at[name], recv_sem=rsem.at[name],
            device_id=dev[to], device_id_type=MESH,
        )

    def start(*names):
        for name in names:
            copy(name).start()

    def got(*names):
        for name in names:
            copy(name).wait_recv()

    def passes(name, *onward):
        got(name)
        start(*onward)

    def pair_terms(logits, positive):
        y = jnp.where(positive, -logits, logits)
        e = jnp.exp(-jnp.abs(y))
        u = 1.0 + e
        r = 1.0 / u
        grad = jnp.where(y >= 0, r, e * r) * scale
        grad = jnp.where(positive, -grad, grad)
        log_term = jnp.where(e < 0.01, e * (1.0 - e * (0.5 - e * (1.0 / 3.0))), jnp.log(u))
        return grad.astype(LOW), jnp.maximum(y, 0.0) + log_term

    def tile(s, c, own):
        texts = pl.ds(pl.multiple_of(c * CHUNK, CHUNK), CHUNK)
        v, t = V[s], T[texts]
        logits = scale * dot(v, t, NT) + bias
        row = lax.broadcasted_iota(jnp.int32, logits.shape, 0)
        col = lax.broadcasted_iota(jnp.int32, logits.shape, 1)
        g, loss = pair_terms(logits, (row == col) & (row < jnp.where(own, ROWS, 0)))
        lacc[...] += jnp.sum(loss.reshape(-1, 8, CHUNK), axis=0)
        gT[texts] += dot(g, v, TN)
        part = dot(g, t, NN)
        gI[s] += part[:ROWS]
        sI[s] += part[ROWS:]

    def send_image(name, s, *more):
        k, h = SUMS[name - name % 2][0], name % 2
        total = gI[s, rows(0, h)] + rI[s, rows(0, h)]
        for m in more:
            got(m + h)
            total += arrived[SUMS[m][0], rows(0, h)].astype(F32)
        out[k, rows(0, h)] = total.astype(LOW)
        start(name)

    def send_text(name, block, *more):
        k, h = SUMS[name - name % 2][0], name % 2
        total = gT[rows(block, h)]
        for m in more:
            got(m + h)
            total += arrived[SUMS[m][0], rows(0, h)].astype(F32)
        out[k, rows(0, h)] = total.astype(LOW)
        start(name)

    for i in range(2):
        loads[i].wait()
        unit[i] = unit_rows(raw[i])[0]
    V[0, :ROWS] = unit[0].astype(LOW)
    T[:ROWS] = unit[1].astype(LOW)
    pl.semaphore_wait(barrier, len(GREETED))
    start(F1 + A, B1 + B, TU + A, TD + B, TX + A, S0 + A)
    start(F1 + B, B1 + A, TU + B, TD + A, TX + B, S0 + B)
    gT[...] = jnp.zeros_like(gT)
    gI[...] = jnp.zeros_like(gI)
    sI[...] = jnp.zeros_like(sI)
    lacc[...] = jnp.zeros_like(lacc)

    passes(F1 + A, F2 + A, S1 + A)
    passes(B1 + B, B2 + B, S2 + B)
    passes(TU + A, T2U + A)
    passes(TD + B, T2D + B)
    passes(TX + A, TXU + A, TXD + A)
    passes(F1 + B, F2 + B, S1 + B)
    passes(B1 + A, B2 + A, S2 + A)
    passes(TX + B, TXU + B, TXD + B)
    got(TU + B, TD + A, S0 + A, S0 + B)

    def serve_0():
        got(S1 + A, S1 + B)

    def serve_1():
        passes(F2 + A, F3 + A, S3 + A)
        passes(B2 + B, B3 + B, S4 + B)
        passes(T2U + A, T3X + A)
        passes(T2D + B, T3X + B)
        got(S2 + A, S2 + B)

    def serve_2():
        passes(F2 + B, F3 + B, S3 + B)
        passes(B2 + A, B3 + A, S4 + A)
        got(S3 + A, S3 + B)

    def serve_3():
        passes(F3 + A, F4 + A, S5 + A)
        passes(B3 + B, B4 + B, S6 + B)
        got(S4 + A, S4 + B)

    def serve_4():
        got(TXU + A, TXD + A, TXU + B, TXD + B, T3X + A, T3X + B)

    def serve_5():
        start(G3)
        passes(F3 + B, S5 + B)
        passes(B3 + A, S6 + A)

    def serve_6():
        start(G4)
        got(S5 + A, S5 + B)
        passes(F4 + A, S7 + A)
        passes(B4 + B, S7 + B)

    def serve_8():
        start(G5)
        got(S7 + A, S7 + B)

    def serve_9():
        got(G5)
        send_image(CF2 + B, 5)

    def serve_10():
        start(G7)
        got(S6 + A, S6 + B)

    def serve_11():
        got(G7)
        send_image(CF3 + A, 7)
        send_image(CB3 + B, 7)

    def serve_12():
        start(G6)
        send_text(Y0U + B, UP)
        send_text(Y0D + A, DOWN)

    def serve_13():
        start(G1)
        got(G6)
        send_image(CB2 + A, 6)
        got(G3)
        send_image(CF1 + B, 3, CF2)

    def serve_14():
        start(G2)
        send_image(CF2 + A, 5, CF3)
        send_image(CB2 + B, 6, CB3)

    def serve_15():
        start(G0)

    served = {
        0: serve_0, 1: serve_1, 2: serve_2, 3: serve_3, 4: serve_4, 5: serve_5, 6: serve_6, 8: serve_8,
        9: serve_9, 10: serve_10, 11: serve_11, 12: serve_12, 13: serve_13, 14: serve_14, 15: serve_15,
    }
    order = ((0, 0), (1, 0), (2, 0), (3, 0), (4, 0), (3, 1), (4, 1), (5, 1),
             (5, 0), (7, 1), (7, 0), (6, 1), (6, 0), (1, 1), (2, 1), (0, 1))

    def picked(i, values):
        number = values[-1]
        for k in range(len(values) - 2, -1, -1):
            number = jnp.where(i == k, values[k], number)
        return number

    def step(i, carry):
        tile(picked(i, [s for s, c in order]), picked(i, [c for s, c in order]), i == 0)
        for k, serve in served.items():
            pl.when(i == k)(serve)
        return carry

    lax.fori_loop(0, len(order), step, 0)

    for h in (A, B):
        send_text(X1 + h, SIDE_FAR)
        send_text(Y1U + h, SIDE_UP)
        send_text(Y1D + h, SIDE_DOWN)
    lout[0] = sum(lacc[:, c : c + 128] for c in range(0, CHUNK, 128))
    start(LC)
    got(G4)
    send_image(CB1 + A, 4, CB2)
    got(G1)
    send_image(CF0 + B, 1, CF1)
    got(LC)
    lout[1] = lout[0] + lin[0]
    start(LX, LM, LF)
    send_image(CF1 + A, 3, CF2)
    send_image(CB1 + B, 4, CB2)
    send_text(Y3U + A, FAR, X1)
    send_text(Y3D + B, FAR, X1)
    got(LX, LM, LF)
    lout[2] = (lout[1] + lin[1]) + (lin[2] + lin[3])
    start(LYU, LYD, LYF)
    got(G2)
    send_image(CB0 + A, 2, CB1)
    send_text(X2 + A, SIDE, Y1U, Y1D)
    send_text(X2 + B, SIDE, Y1U, Y1D)
    got(LYU, LYD, LYF)
    lout[3] = (lout[2] + lin[6]) + (lin[4] + lin[5])
    start(LZ)
    send_image(CF0 + A, 1, CF1)
    send_image(CB0 + B, 2, CB1)
    send_text(Y0U + A, UP, Y3U)
    send_text(Y0D + B, DOWN, Y3D)
    got(LZ)
    lout[4] = lout[3] + lin[7]
    start(LZU, LZD, LZF)

    def finish(i, total, ref, *more):
        for m in more:
            got(m + A, m + B)
            total += arrived[SUMS[m][0]].astype(F32)
        ref[...] = back_norm(unit[i], unit_rows(raw[i])[1], total)

    got(G0)
    finish(0, gI[0] + rI[0], gimg_ref, CF0, CB0)
    finish(1, gT[:ROWS], gtxt_ref, X2, Y0U, Y0D)
    got(LZU, LZD, LZF)
    total = (lout[4] + lin[10]) + (lin[8] + lin[9])
    batch = ROWS * lax.axis_size("group") * lax.axis_size("loop")
    loss_ref[...] = jnp.sum(total, keepdims=True).reshape(1, 1) / batch
    for name in SENT:
        copy(name).wait_send()


def body(images, texts, logit_scale, logit_bias):
    vmem = pl.BlockSpec(memory_space=pltpu.VMEM)
    smem = pl.BlockSpec(memory_space=pltpu.SMEM)
    hbm = pl.BlockSpec(memory_space=pl.ANY)
    block = (ROWS, WIDTH)
    loss, grad_images, grad_texts = pl.pallas_call(
        kernel,
        out_shape=(
            jax.ShapeDtypeStruct((1, 1), F32),
            jax.ShapeDtypeStruct(block, F32),
            jax.ShapeDtypeStruct(block, F32),
        ),
        in_specs=[smem, smem, hbm, hbm],
        out_specs=(vmem, vmem, vmem),
        scratch_shapes=[
            pltpu.VMEM((2,) + block, LOW),
            pltpu.VMEM((2,) + block, F32),
            pltpu.VMEM((8, 2 * ROWS, WIDTH), LOW),
            pltpu.VMEM((8 * ROWS, WIDTH), LOW),
            pltpu.VMEM((8,) + block, F32),
            pltpu.VMEM((8,) + block, F32),
            pltpu.VMEM((8,) + block, F32),
            pltpu.VMEM((8 * ROWS, WIDTH), F32),
            pltpu.VMEM((15,) + block, LOW),
            pltpu.VMEM((15,) + block, LOW),
            pltpu.VMEM((8, CHUNK), F32),
            pltpu.VMEM((5, 8, 128), F32),
            pltpu.VMEM((11, 8, 128), F32),
            pltpu.SemaphoreType.DMA((2,)),
            pltpu.SemaphoreType.DMA((LAST,)),
            pltpu.SemaphoreType.DMA((LAST,)),
        ],
        compiler_params=pltpu.CompilerParams(
            collective_id=0, has_side_effects=True, vmem_limit_bytes=60 * 2**20
        ),
    )(logit_scale, logit_bias, images, texts)
    return loss.reshape(()), grad_images, grad_texts


def solution(mesh):
    rows = P(("group", "loop"), None)
    return jax.shard_map(
        body,
        mesh=mesh,
        in_specs=(rows, rows, P(), P()),
        out_specs=(P(), rows, rows),
        check_vma=False,
    )
```

time: 354 us -> 93.4 us (0.26); the launches traced: 350 us -> 93.2 us
  matrix products: 142 us -> 0 us
  waiting for transfers between devices: 89.2 us -> 0 us
  Pallas kernels: 0 us -> 86.7 us
  blocking collectives: 79.8 us -> 0 us
  between operations: 15.9 us -> 3.67 us
  other arithmetic: 9.74 us -> 0 us
  starting transfers between devices: 7.31 us -> 0 us
  loops' own time: 5.64 us -> 0 us
    dot_general x24 -> x0, matrix products: 142 us -> none  [the longest x8 72.7 us: one_step(): jnp.dot(pair_grad, visitor, preferred_element_type=jnp.float32)]
    pallas_call x0 -> x1, Pallas kernels: none -> 86.7 us  [body(): pl.pallas_call(kernel, out_shape=(jax.ShapeDtypeStruct((1, 1), F32), jax....]
    psum x1 -> x0, blocking collectives: 79.8 us -> none  [body(): total = lax.psum(loss_acc, ('group', 'loop'))]
    ppermute x17 -> x0, waiting for transfers between devices: 48.2 us -> none  [passed_along(): return lax.ppermute(block, axis, route)]
    all_gather x1 -> x0, waiting for transfers between devices: 41 us -> none  [body(): text_rows = lax.all_gather(text_low, 'group', axis=0, tiled=True)]
    ppermute x17 -> x0, starting transfers between devices: 7.23 us -> none  [passed_along(): return lax.ppermute(block, axis, route)]
    another operation x1 -> x0, loops' own time: 5.64 us -> none  [body(): final = lax.fori_loop(0, half_loop, one_step, start_carry)]
    reduce_sum x4 -> x0, other arithmetic: 3.74 us -> none  [the longest x2 2.21 us: unit_rows(): norm = jnp.sqrt(jnp.sum(wide * wide, axis=1, keepdims=True) + 1e-06)]
  transfers between devices with their start and end apart: 19 -> 0, of which waited for: 9 -> 0; matrix products, arithmetic and copies ran while one was open for 42% -> 0% of each run, Pallas kernels for 0% -> 0%
where the time goes in v1:
time: 93.4 us; the launch traced here: 93.2 us
  Pallas kernels  86.7 us (93%)
  between operations  3.67 us (4%)
  local copies, waits for them, and re-layouts  2.8 us (3%)
    pallas_call x1, Pallas kernels, body(): pl.pallas_call(kernel, out_shape=(jax.ShapeDtypeStruct((1, 1), F32), jax....  86.7 us
    unnamed x4, local copies, waits for them, and re-layouts  2.8 us

profile of v1, /device:TPU:16, one launch (start us, length us, event | category | flops | bytes accessed | tf_op | source)
XLA Modules:
  0.0 93.2 jit_solution(5239615111878632465)
XLA Ops:
  1.9 86.7 %shard_map.67 = (f32[1,1]{1,0:T(1,128)}, f32[128,1152]{1,0:T(8,128)}, f32[128,1152]{1,0:T(8,128)}) custom-call(f32[1]{0:T(128)S(6)} %copy.10.scale_ref, f32[1]{0:T(128)S(6)} %copy.11.bias_ref, bf16[128,1152]{1,0:T(8,128)(2,1)} %img_ref.1, bf16[128,1152]{1,0:T(8,128)(2,1)} %txt_ref.1), custom_call_target="tpu_custom_call" | custom-call | tf_op jit(solution)/shard_map/pallas_call | solution.py:372
  89.3 0.0 copy-start
  89.3 2.0 %copy.13 = f32[128,1152]{1,0:T(8,128)} copy(f32[128,1152]{1,0:T(8,128)} %get-tuple-element.13) | data formatting | bytes 1179648
  91.2 0.0 copy-done
  91.3 0.8 copy.14
Async XLA Ops:
  89.3 2.0 %copy-start = (f32[128,1152]{1,0:T(8,128)S(1)}, f32[128,1152]{1,0:T(8,128)}, u32[]{:S(2)}) copy-start(f32[128,1152]{1,0:T(8,128)} %get-tuple-element.14) | copy-start | bytes 1769476

commit v2 on v1

v2 whole, which is shorter than its diff:
```python
import jax
import jax.numpy as jnp
from jax import lax
from jax.experimental import pallas as pl
from jax.experimental.pallas import tpu as pltpu
from jax.sharding import PartitionSpec as P

MESH = pl.DeviceIdType.MESH
F32 = jnp.float32
LOW = jnp.bfloat16
ROWS = 128
HALF = 64
WIDTH = 1152
CHUNK = 4 * ROWS
NT = (((1,), (1,)), ((), ()))
NN = (((1,), (0,)), ((), ()))
TN = (((0,), (0,)), ((), ()))
A, B = 0, 1
(
    NEXT, PREV, BACK, UNBACK, YUP, YDOWN, YFAR, CORE, LO, MIRROR, XFAR, ZPAIR, Z2, Z4, Z6, DEVICES,
) = range(16)
(
    F1, F2, F3, F4, B1, B2, B3, B4, S0, S1, S2, S3, S4, S5, S6, S7, G0, G1, G2, G3, G4, G5, G6, G7,
    TU, TD, TX, TXU, TXD, T2, T3X, CF0, CF1, CF2, CF3, CB0, CB1, CB2, CB3,
    X1, X2, Y1U, Y1D, Y0U, Y0D, Y3U, Y3D,
    LOSS,
) = range(0, 96, 2)
LAST = LOSS + 11
HALVED = (
    F1, F2, F3, B1, B2, B3, S0, S1, S2, S3, S4, S5, S6, S7, TU, TD, TX, TXU, TXD, T2, T3X,
    CF0, CF1, CF2, CB0, CB1, CB2, X1, X2, Y1U, Y1D, Y0U, Y0D,
)
SENT = (
    [hop + h for hop in HALVED for h in (A, B)]
    + [F4 + A, B4 + B, CF3 + A, CB3 + B, Y3U + A, Y3D + B]
    + list(range(G0, G7 + 1, 2))
    + list(range(LOSS, LAST))
)
VISITS = {
    F1: (0, 1, NEXT), F2: (1, 3, NEXT), F3: (3, 5, NEXT), F4: (5, 7, NEXT),
    B1: (0, 2, BACK), B2: (2, 4, PREV), B3: (4, 6, PREV), B4: (6, 7, PREV),
}
OWN, SIDE, UP, DOWN, FAR, SIDE_UP, SIDE_DOWN, SIDE_FAR = range(8)
TEXTS = {
    TU: (OWN, DOWN, YUP), TD: (OWN, UP, YDOWN), TX: (OWN, SIDE, LO),
    T2: (OWN, FAR, YFAR),
    TXU: (SIDE, SIDE_DOWN, YUP), TXD: (SIDE, SIDE_UP, YDOWN), T3X: (FAR, SIDE_FAR, LO),
}
SUMS = {
    CF0: (0, PREV), CF1: (1, PREV), CF2: (2, PREV), CF3: (3, PREV),
    CB0: (4, UNBACK), CB1: (5, NEXT), CB2: (6, NEXT), CB3: (7, NEXT),
    X1: (8, LO), X2: (9, LO), Y1U: (10, YUP), Y1D: (11, YDOWN),
    Y0U: (12, YUP), Y0D: (13, YDOWN), Y3U: (14, YUP), Y3D: (14, YDOWN),
}
ROUNDS = (
    (CORE,),
    (LO, XFAR, MIRROR),
    (YFAR, YUP, YDOWN),
    (ZPAIR,),
    (Z4, Z2, Z6),
)
LOSSES = [(r, to) for r, partners in enumerate(ROUNDS) for to in partners]


def dot(a, b, dims):
    return lax.dot_general(a, b, dims, preferred_element_type=F32)


def unit_rows(raw):
    wide = raw.astype(F32)
    norm = jnp.sqrt(jnp.sum(wide * wide, axis=1, keepdims=True) + 1e-06)
    return wide / norm, norm


def back_norm(unit, norm, grad):
    return (grad - unit * jnp.sum(unit * grad, axis=1, keepdims=True)) / norm


def devices():
    g, l = lax.axis_index("group"), lax.axis_index("loop")
    core, y, lo = g % 2, (g // 2) % 4, g // 8
    z, hi = l % 8, l // 8

    def at(lo=lo, y=y, core=core, hi=hi, z=z):
        return ((lo * 4 + y) * 2 + core, hi * 8 + z)

    def flip(bit, when):
        return jnp.where(when, 1 - bit, bit)

    up, down = (z + 1) % 8, (z + 7) % 8
    return {
        NEXT: at(lo=flip(lo, z == 7), hi=flip(hi, z == 7), z=up),
        PREV: at(lo=flip(lo, z == 0), hi=flip(hi, z == 0), z=down),
        BACK: at(lo=flip(lo, z != 0), hi=flip(hi, z != 0), z=down),
        UNBACK: at(lo=flip(lo, z != 7), hi=flip(hi, z != 7), z=up),
        YUP: at(y=(y + 1) % 4),
        YDOWN: at(y=(y + 3) % 4),
        YFAR: at(y=(y + 2) % 4),
        CORE: at(core=1 - core),
        LO: at(lo=1 - lo),
        MIRROR: at(lo=1 - lo, hi=1 - hi),
        XFAR: at(hi=1 - hi),
        ZPAIR: at(z=z + 1 - 2 * (z % 2)),
        Z2: at(z=(z + 2) % 8),
        Z4: at(z=(z + 4) % 8),
        Z6: at(z=(z + 6) % 8),
    }


def kernel(
    scale_ref, bias_ref, img_ref, txt_ref, loss_ref, gimg_ref, gtxt_ref,
    raw, unit, V, T, gI, sI, rI, gT, out, arrived, lacc, lout, lin, lsem, ssem, rsem,
):
    dev = devices()
    scale, bias = scale_ref[0], bias_ref[0]
    loads = [pltpu.make_async_copy(ref, raw.at[i], lsem.at[i]) for i, ref in enumerate((img_ref, txt_ref))]
    for load in loads:
        load.start()

    barrier = pltpu.get_barrier_semaphore()
    for to in range(DEVICES):
        pl.semaphore_signal(barrier, inc=1, device_id=dev[to], device_id_type=MESH)

    def rows(i, h):
        return pl.ds(i * ROWS + h * HALF, HALF)

    def copy(name):
        h, base = name % 2, name - name % 2
        if name >= LOSS:
            r, to = LOSSES[name - LOSS]
            src, dst = lout.at[r], lin.at[name - LOSS]
        elif base in VISITS:
            s, d, to = VISITS[base]
            src, dst = V.at[s, rows(0, h)], V.at[d, rows(0, h)]
        elif base in TEXTS:
            s, d, to = TEXTS[base]
            src, dst = T.at[rows(s, h)], T.at[rows(d, h)]
        elif base in SUMS:
            k, to = SUMS[base]
            src, dst = out.at[k, rows(0, h)], arrived.at[k, rows(0, h)]
        elif base >= G0:
            s, to = (base - G0) // 2, CORE
            src, dst = sI.at[s], rI.at[s]
        else:
            s, to = (base - S0) // 2, CORE
            src, dst = V.at[s, rows(0, h)], V.at[s, rows(1, h)]
        return pltpu.make_async_remote_copy(
            src_ref=src, dst_ref=dst, send_sem=ssem.at[name], recv_sem=rsem.at[name],
            device_id=dev[to], device_id_type=MESH,
        )

    def start(*names):
        for name in names:
            copy(name).start()

    def got(*names):
        for name in names:
            copy(name).wait_recv()

    def passes(name, *onward):
        got(name)
        start(*onward)

    def pair_terms(logits):
        w = jnp.exp(jnp.minimum(logits, 80.0))
        u = 1.0 + w
        prob = w * (1.0 / u)
        log_term = jnp.where(w < 0.01, w * (1.0 - w * (0.5 - w * (1.0 / 3.0))), jnp.log(u))
        return prob, jnp.maximum(logits, log_term)

    def tile(s, texts, own=False):
        v, t = V[s], T[texts]
        logits = scale * dot(v, t, NT) + bias
        if own:
            row = lax.broadcasted_iota(jnp.int32, logits.shape, 0)
            col = lax.broadcasted_iota(jnp.int32, logits.shape, 1)
            positive = (row == col) & (row < ROWS)
            prob, loss = pair_terms(jnp.where(positive, -logits, logits))
            prob = jnp.where(positive, -prob, prob)
        else:
            prob, loss = pair_terms(logits)
        g = (prob * scale).astype(LOW)
        lacc[:, : t.shape[0]] += jnp.sum(loss.reshape(-1, 8, t.shape[0]), axis=0)
        gT[texts] += dot(g, v, TN)
        return dot(g, t, NN)

    def half_tile(s, c, own=False):
        part = tile(s, pl.ds(pl.multiple_of(c * CHUNK, CHUNK), CHUNK), own)
        gI[s] += part[:ROWS]
        sI[s] += part[ROWS:]

    def whole_tile(s):
        part = tile(s, pl.ds(0, 2 * CHUNK))
        gI[s] = part[:ROWS]
        sI[s] = part[ROWS:]

    def send_image(name, s, *more):
        k, h = SUMS[name - name % 2][0], name % 2
        total = gI[s, rows(0, h)] + rI[s, rows(0, h)]
        for m in more:
            got(m + h)
            total += arrived[SUMS[m][0], rows(0, h)].astype(F32)
        out[k, rows(0, h)] = total.astype(LOW)
        start(name)

    def send_text(name, block, *more):
        k, h = SUMS[name - name % 2][0], name % 2
        total = gT[rows(block, h)]
        for m in more:
            got(m + h)
            total += arrived[SUMS[m][0], rows(0, h)].astype(F32)
        out[k, rows(0, h)] = total.astype(LOW)
        start(name)

    for i in range(2):
        loads[i].wait()
        unit[i] = unit_rows(raw[i])[0]
    V[0, :ROWS] = unit[0].astype(LOW)
    T[:ROWS] = unit[1].astype(LOW)
    pl.semaphore_wait(barrier, DEVICES)
    start(F1 + A, B1 + B, TU + A, TD + B, TX + A, S0 + A)
    start(F1 + B, B1 + A, TU + B, TD + A, TX + B, S0 + B)
    start(T2 + A, T2 + B)
    gT[...] = jnp.zeros_like(gT)
    gI[:5] = jnp.zeros_like(gI[:5])
    sI[:5] = jnp.zeros_like(sI[:5])
    lacc[...] = jnp.zeros_like(lacc)

    passes(F1 + A, F2 + A, S1 + A)
    passes(B1 + B, B2 + B, S2 + B)
    got(TU + A, TD + B, TU + B, TD + A, S0 + A, S0 + B)
    passes(TX + A, TXU + A, TXD + A)
    passes(TX + B, TXU + B, TXD + B)
    half_tile(0, 0, True)
    passes(F1 + B, F2 + B, S1 + B)
    passes(B1 + A, B2 + A, S2 + A)
    got(S1 + A, S1 + B)

    def after_1():
        passes(T2 + A, T3X + A)
        passes(T2 + B, T3X + B)
        passes(F2 + A, F3 + A, S3 + A)
        passes(B2 + B, B3 + B, S4 + B)
        got(S2 + A, S2 + B)

    def after_2():
        passes(F2 + B, F3 + B, S3 + B)
        passes(B2 + A, B3 + A, S4 + A)
        got(S3 + A, S3 + B)

    def after_3():
        passes(F3 + A, F4 + A, S5 + A)
        passes(B3 + B, B4 + B, S6 + B)
        got(S4 + A, S4 + B)

    def after_4():
        got(TXU + A, TXD + A, TXU + B, TXD + B, T3X + A, T3X + B)

    def after_5():
        start(G0)
        passes(F3 + B, S5 + B)
        passes(B3 + A, S6 + A)

    def after_6():
        start(G1)

    def after_7():
        start(G2)
        passes(F4 + A, S7 + A)
        passes(B4 + B, S7 + B)
        got(S5 + A, S5 + B)

    def after_8():
        start(G5)
        got(S7 + A, S7 + B)

    def after_9():
        start(G7)
        got(G5)
        send_image(CF2 + B, 5)

    def after_10():
        start(G3)
        got(G7)
        send_image(CF3 + A, 7)
        send_image(CB3 + B, 7)
        got(S6 + A, S6 + B)

    def after_11():
        start(G6)

    def after_12():
        start(G4)
        got(G6)
        send_image(CB2 + A, 6)

    order = (
        (1, 0, after_1), (2, 0, after_2), (3, 0, after_3), (4, 0, after_4), (0, 1, after_5), (1, 1, after_6),
        (2, 1, after_7), (5, 2, after_8), (7, 2, after_9), (3, 1, after_10), (6, 2, after_11), (4, 1, after_12),
    )

    def step(i, carry):
        s, c = order[-1][:2]
        for k, entry in enumerate(order[:-1]):
            s = jnp.where(i == k, entry[0], s)
            c = jnp.where(i == k, entry[1], c)
        pl.when(c < 2)(lambda: half_tile(s, c))
        pl.when(c == 2)(lambda: whole_tile(s))
        for k, entry in enumerate(order):
            pl.when(i == k)(entry[2])
        return carry

    lax.fori_loop(0, len(order), step, 0)

    def loss_terms(r):
        names = [LOSS + i for i, entry in enumerate(LOSSES) if entry[0] == r]
        got(*names)
        terms = [lout[r]] + [lin[name - LOSS] for name in names]
        while len(terms) > 1:
            terms = [a + b for a, b in zip(terms[::2], terms[1::2])]
        return terms[0]

    def send_loss(r, total):
        lout[r] = total
        start(*[LOSS + i for i, entry in enumerate(LOSSES) if entry[0] == r])

    for h in (A, B):
        send_text(X1 + h, SIDE_FAR)
    for h in (A, B):
        send_text(Y1U + h, SIDE_UP)
        send_text(Y1D + h, SIDE_DOWN)
    send_loss(0, sum(lacc[:, c : c + 128] for c in range(0, 2 * CHUNK, 128)))
    send_image(CF2 + A, 5, CF3)
    send_loss(1, loss_terms(0))
    send_image(CB2 + B, 6, CB3)
    got(G1, G2, G3, G4)
    send_image(CF1 + B, 3, CF2)
    send_text(Y3U + A, FAR, X1)
    send_text(X2 + A, SIDE, Y1U, Y1D)
    send_loss(2, loss_terms(1))
    send_image(CB1 + A, 4, CB2)
    send_text(Y3D + B, FAR, X1)
    send_text(Y0U + B, UP)
    send_text(Y0D + A, DOWN)
    send_image(CF1 + A, 3, CF2)
    send_image(CB1 + B, 4, CB2)
    send_loss(3, loss_terms(2))
    send_text(X2 + B, SIDE, Y1U, Y1D)
    send_image(CF0 + B, 1, CF1)
    send_image(CB0 + A, 2, CB1)
    send_loss(4, loss_terms(3))
    send_text(Y0U + A, UP, Y3U)
    send_text(Y0D + B, DOWN, Y3D)
    send_image(CF0 + A, 1, CF1)
    send_image(CB0 + B, 2, CB1)

    def finish(i, total, ref, *more):
        for m in more:
            got(m + A, m + B)
            total += arrived[SUMS[m][0]].astype(F32)
        ref[...] = back_norm(unit[i], unit_rows(raw[i])[1], total)

    got(G0)
    finish(0, gI[0] + rI[0], gimg_ref, CF0, CB0)
    finish(1, gT[:ROWS], gtxt_ref, X2, Y0U, Y0D)
    total = loss_terms(4)
    batch = ROWS * lax.axis_size("group") * lax.axis_size("loop")
    loss_ref[...] = jnp.sum(total, keepdims=True).reshape(1, 1) / batch
    for name in SENT:
        copy(name).wait_send()


def body(images, texts, logit_scale, logit_bias):
    vmem = pl.BlockSpec(memory_space=pltpu.VMEM)
    smem = pl.BlockSpec(memory_space=pltpu.SMEM)
    hbm = pl.BlockSpec(memory_space=pl.ANY)
    block = (ROWS, WIDTH)
    loss, grad_images, grad_texts = pl.pallas_call(
        kernel,
        out_shape=(
            jax.ShapeDtypeStruct((1, 1), F32),
            jax.ShapeDtypeStruct(block, F32),
            jax.ShapeDtypeStruct(block, F32),
        ),
        in_specs=[smem, smem, hbm, hbm],
        out_specs=(vmem, vmem, vmem),
        scratch_shapes=[
            pltpu.VMEM((2,) + block, LOW),
            pltpu.VMEM((2,) + block, F32),
            pltpu.VMEM((8, 2 * ROWS, WIDTH), LOW),
            pltpu.VMEM((8 * ROWS, WIDTH), LOW),
            pltpu.VMEM((8,) + block, F32),
            pltpu.VMEM((8,) + block, F32),
            pltpu.VMEM((8,) + block, F32),
            pltpu.VMEM((8 * ROWS, WIDTH), F32),
            pltpu.VMEM((15,) + block, LOW),
            pltpu.VMEM((15,) + block, LOW),
            pltpu.VMEM((8, 2 * CHUNK), F32),
            pltpu.VMEM((len(ROUNDS), 8, 128), F32),
            pltpu.VMEM((len(LOSSES), 8, 128), F32),
            pltpu.SemaphoreType.DMA((2,)),
            pltpu.SemaphoreType.DMA((LAST,)),
            pltpu.SemaphoreType.DMA((LAST,)),
        ],
        compiler_params=pltpu.CompilerParams(
            collective_id=0, has_side_effects=True, vmem_limit_bytes=60 * 2**20
        ),
    )(logit_scale, logit_bias, images, texts)
    return loss.reshape(()), grad_images, grad_texts


def solution(mesh):
    rows = P(("group", "loop"), None)
    return jax.shard_map(
        body,
        mesh=mesh,
        in_specs=(rows, rows, P(), P()),
        out_specs=(P(), rows, rows),
        check_vma=False,
    )
```

time: 93.4 us -> 91.3 us (0.978); the launches traced: 93.2 us -> 89.8 us
  Pallas kernels: 86.7 us -> 83.3 us
    pallas_call x1, Pallas kernels: 86.7 us -> 83.3 us  [body(): pl.pallas_call(kernel, out_shape=(jax.ShapeDtypeStruct((1, 1), F32), jax....]
where the time goes in v2:
time: 91.3 us; the launch traced here: 89.8 us
  Pallas kernels  83.3 us (91%)
  between operations  3.67 us (4%)
  local copies, waits for them, and re-layouts  2.8 us (3%)
    pallas_call x1, Pallas kernels, body(): pl.pallas_call(kernel, out_shape=(jax.ShapeDtypeStruct((1, 1), F32), jax....  83.3 us
    unnamed x4, local copies, waits for them, and re-layouts  2.8 us

profile of v2, /device:TPU:16, one launch (start us, length us, event | category | flops | bytes accessed | tf_op | source)
XLA Modules:
  0.0 89.8 jit_solution(6310086709536557683)
XLA Ops:
  1.9 83.3 %shard_map.67 = (f32[1,1]{1,0:T(1,128)}, f32[128,1152]{1,0:T(8,128)}, f32[128,1152]{1,0:T(8,128)}) custom-call(f32[1]{0:T(128)S(6)} %copy.10.scale_ref, f32[1]{0:T(128)S(6)} %copy.11.bias_ref, bf16[128,1152]{1,0:T(8,128)(2,1)} %img_ref.1, bf16[128,1152]{1,0:T(8,128)(2,1)} %txt_ref.1), custom_call_target="tpu_custom_call" | custom-call | tf_op jit(solution)/shard_map/pallas_call | solution.py:378
  85.9 0.0 copy-start
  85.9 2.0 %copy.13 = f32[128,1152]{1,0:T(8,128)} copy(f32[128,1152]{1,0:T(8,128)} %get-tuple-element.13) | data formatting | bytes 1179648
  87.9 0.0 copy-done
  87.9 0.8 copy.14
Async XLA Ops:
  85.9 2.0 %copy-start = (f32[128,1152]{1,0:T(8,128)S(1)}, f32[128,1152]{1,0:T(8,128)}, u32[]{:S(2)}) copy-start(f32[128,1152]{1,0:T(8,128)} %get-tuple-element.14) | copy-start | bytes 1769476

commit v3 on v2

--- a/solution.py
+++ b/solution.py
@@ -360,14 +360,14 @@
             total += arrived[SUMS[m][0]].astype(F32)
         ref[...] = back_norm(unit[i], unit_rows(raw[i])[1], total)
 
-    got(G0)
-    finish(0, gI[0] + rI[0], gimg_ref, CF0, CB0)
     finish(1, gT[:ROWS], gtxt_ref, X2, Y0U, Y0D)
     total = loss_terms(4)
     batch = ROWS * lax.axis_size("group") * lax.axis_size("loop")
     loss_ref[...] = jnp.sum(total, keepdims=True).reshape(1, 1) / batch
     for name in SENT:
         copy(name).wait_send()
+    got(G0)
+    finish(0, gI[0] + rI[0], gimg_ref, CF0, CB0)
 
 
 def body(images, texts, logit_scale, logit_bias):

time: 91.3 us -> 90.8 us (level)
  no operation moved by 1% of the time
where the time goes in v3:
time: 90.8 us; the launch traced here: 89.8 us
  Pallas kernels  83.3 us (92%)
  between operations  3.67 us (4%)
  local copies, waits for them, and re-layouts  2.8 us (3%)
    pallas_call x1, Pallas kernels, body(): pl.pallas_call(kernel, out_shape=(jax.ShapeDtypeStruct((1, 1), F32), jax....  83.3 us
    unnamed x4, local copies, waits for them, and re-layouts  2.8 us

profile of v3, /device:TPU:16, one launch (start us, length us, event | category | flops | bytes accessed | tf_op | source)
XLA Modules:
  0.0 89.8 jit_solution(4184949689884824520)
XLA Ops:
  1.9 83.3 %shard_map.67 = (f32[1,1]{1,0:T(1,128)}, f32[128,1152]{1,0:T(8,128)}, f32[128,1152]{1,0:T(8,128)}) custom-call(f32[1]{0:T(128)S(6)} %copy.10.scale_ref, f32[1]{0:T(128)S(6)} %copy.11.bias_ref, bf16[128,1152]{1,0:T(8,128)(2,1)} %img_ref.1, bf16[128,1152]{1,0:T(8,128)(2,1)} %txt_ref.1), custom_call_target="tpu_custom_call" | custom-call | tf_op jit(solution)/shard_map/pallas_call | solution.py:378
  85.8 0.0 copy-start
  85.9 2.0 %copy.13 = f32[128,1152]{1,0:T(8,128)} copy(f32[128,1152]{1,0:T(8,128)} %get-tuple-element.13) | data formatting | bytes 1179648
  87.8 0.0 copy-done
  87.8 0.8 copy.14
Async XLA Ops:
  85.8 2.0 %copy-start = (f32[128,1152]{1,0:T(8,128)S(1)}, f32[128,1152]{1,0:T(8,128)}, u32[]{:S(2)}) copy-start(f32[128,1152]{1,0:T(8,128)} %get-tuple-element.14) | copy-start | bytes 1769476
